TPU v7x, 32 devices: a whole 2x2x4 slice. The times are simulated.
32 devices in a mesh: groups: 2 (over x), seq: 16 (over z, y, core).
Axes of the slice: x: 2, y: 2, z: 4, core: 2. Of those that a mesh axis runs over, the one named last changes fastest.
Arguments:
- tiles: bfloat16 [1024, 16, 1536], P(('groups', 'seq')), parts along dimension 0, may hold values from -6 to 6
- tile_gain: bfloat16 [1536], replicated, may hold values from 0.099609375 to 1.8984375
- w_query: bfloat16 [1536, 768], P('seq'), may hold values from -3 to 3
- w_key: bfloat16 [1536, 768], P('seq'), may hold values from -3 to 3
- w_value: bfloat16 [1536, 768], P('seq'), may hold values from -0.15625 to 0.15625
- w_out: bfloat16 [768, 1536], P('seq'), may hold values from -0.21875 to 0.21875
- pool_gain: bfloat16 [1536], replicated, may hold values from 0.099609375 to 1.8984375
- w_in: bfloat16 [1536, 768], P('seq'), may hold values from -0.15625 to 0.15625
- block_order: int32 [256], P('groups'), parts along dimension 0, may hold values from 0 to 127, each once
- slide_gain: bfloat16 [768], replicated, may hold values from 0.099609375 to 1.8984375
- w_sq: bfloat16 [768, 768], P('seq'), may hold values from -3 to 3
- w_sk: bfloat16 [768, 768], P('seq'), may hold values from -3 to 3
- w_sv: bfloat16 [768, 768], P('seq'), may hold values from -0.21875 to 0.21875
- w_so: bfloat16 [768, 768], P('seq'), may hold values from -0.21875 to 0.21875
Outputs:
- slide_out: bfloat16 [1024, 768], P(('groups', 'seq')), parts along dimension 0
There are 2 independent parts, one for each index of `groups`. A program takes and returns all parts, laid end to end along the dimension named above; an argument that names none is the same for every part. Nothing has to cross between parts.
Inputs may be any that keep to these rules, and one draw needn't show every extreme that they name: block_order is a permutation of 0 to 127.
All inputs are finite; a program needn't handle non-finite values.
Results may differ from a plain program's by a relative error of at most 0.0085.
Values may be sent and summed in bfloat16 or wider, within the bound.
A program may use at most 128 MiB of HBM per device.

v0:
```python
import jax
import jax.numpy as jnp
from jax import lax
from jax.sharding import PartitionSpec as P

HT = 12
HD = 64
HS = 12


epsilon = 1e-06
scaling = 0.125


def partner(value, axis, apart):
    mask = 2**apart
    pairs = [(source, source ^ mask) for source in range(lax.axis_size(axis))]
    return lax.ppermute(value, axis, pairs)


def norm_rows(rows, gain):
    values = rows.astype(jnp.float32)
    centred = values - jnp.mean(values, axis=-1, keepdims=True)
    spread = jnp.mean(centred * centred, axis=-1, keepdims=True)
    return centred * lax.rsqrt(spread + epsilon) * gain.astype(jnp.float32)


def select_rows(rows, chosen, dilation):
    row_total, head_total, head_width = rows.shape
    grouped = rows.reshape(row_total // dilation, dilation, head_total, head_width)
    return jnp.sum(jnp.where(chosen[None, :, :, None], grouped, jnp.zeros((), rows.dtype)), axis=1)


def add_products(operands, shard_rows):
    return tuple(
        (
            jnp.dot(operand, weight_rows, preferred_element_type=jnp.float32)
            for operand, weight_rows in zip(operands, shard_rows)
        )
    )


def shards(
    tiles,
    tile_gain,
    w_query,
    w_key,
    w_value,
    w_out,
    pool_gain,
    w_in,
    block_order,
    slide_gain,
    w_sq,
    w_sk,
    w_sv,
    w_so,
):
    tile_count, patch_count, model_width = tiles.shape
    row_count = tile_count * patch_count
    inner_width = w_query.shape[1]
    normed = norm_rows(tiles, tile_gain).astype(jnp.bfloat16).reshape(row_count, model_width)
    projected = add_products(
        (normed, normed, normed),
        (
            lax.all_gather(w_query, "seq", axis=0, tiled=True),
            lax.all_gather(w_key, "seq", axis=0, tiled=True),
            lax.all_gather(w_value, "seq", axis=0, tiled=True),
        ),
    )
    tile_query, tile_keys, tile_values = (
        matrix.astype(jnp.bfloat16).reshape(tile_count, patch_count, HT, HD) for matrix in projected
    )
    scores = (
        jnp.einsum("tqhd,tkhd->thqk", tile_query, tile_keys, preferred_element_type=jnp.float32)
        * scaling
    )
    row_max = jnp.max(scores, axis=-1, keepdims=True)
    weights = jnp.exp(scores - row_max)
    totals = jnp.sum(weights, axis=-1)
    attended = jnp.einsum(
        "thqk,tkhd->tqhd",
        weights.astype(jnp.bfloat16),
        tile_values,
        preferred_element_type=jnp.float32,
    )
    attended = (attended / jnp.transpose(totals, (0, 2, 1))[..., None]).astype(jnp.bfloat16)
    attended_mean = jnp.mean(
        attended.reshape(tile_count, patch_count, inner_width), axis=1, dtype=jnp.float32
    )
    token_mean = jnp.mean(tiles, axis=1, dtype=jnp.float32)
    out_term = jnp.dot(
        attended_mean,
        lax.all_gather(w_out, "seq", axis=0, tiled=True).astype(jnp.float32),
        precision=lax.Precision.HIGHEST,
    )
    pooled = token_mean + out_term
    pooled_norm = norm_rows(pooled, pool_gain).astype(jnp.bfloat16)
    embedding = add_products((pooled_norm,), (lax.all_gather(w_in, "seq", axis=0, tiled=True),))[0]
    embedding = embedding.astype(jnp.bfloat16)
    position = lax.axis_index("seq")
    seq_size = lax.axis_size("seq")
    gathered = lax.all_gather(embedding, "seq", axis=0, tiled=True)
    slide_width = gathered.shape[1]
    block_count = block_order.shape[0]
    block_len = gathered.shape[0] // block_count
    blocks = gathered.reshape(block_count, block_len, slide_width)
    per_device = tile_count // block_len
    wanted = lax.dynamic_slice_in_dim(block_order, position * per_device, per_device)
    own_rows = jnp.take(blocks, wanted, axis=0).reshape(per_device * block_len, slide_width)
    own_norm = norm_rows(own_rows, slide_gain).astype(jnp.bfloat16)
    total_rows = seq_size * tile_count
    source_rows = own_norm.shape[0]
    slide_proj = add_products(
        (own_norm, own_norm, own_norm),
        (
            lax.all_gather(w_sq, "seq", axis=0, tiled=True),
            lax.all_gather(w_sk, "seq", axis=0, tiled=True),
            lax.all_gather(w_sv, "seq", axis=0, tiled=True),
        ),
    )
    slide_query = slide_proj[0].astype(jnp.bfloat16).reshape(tile_count, HS, HD)
    slide_keys = slide_proj[1].astype(jnp.bfloat16).reshape(source_rows, HS, HD)
    slide_values = slide_proj[2].astype(jnp.bfloat16).reshape(source_rows, HS, HD)
    head_ids = jnp.arange(HS)
    local_ids = jnp.arange(tile_count)
    level_outs = []
    level_lses = []
    level_masks = []
    for seg_len, dilation in ((total_rows // 4, 1), (total_rows // 2, 2), (total_rows, 4)):
        chosen = jnp.arange(dilation)[:, None] == head_ids[None, :] % dilation
        seg_keys = select_rows(slide_keys, chosen, dilation)
        seg_values = select_rows(slide_values, chosen, dilation)
        for bit_number in range((seg_len // tile_count).bit_length() - 1):
            other_keys, other_values = partner((seg_keys, seg_values), "seq", bit_number)
            low_half = position >> bit_number & 1 == 0
            seg_keys = jnp.where(
                low_half,
                jnp.concatenate([seg_keys, other_keys], 0),
                jnp.concatenate([other_keys, seg_keys], 0),
            )
            seg_values = jnp.where(
                low_half,
                jnp.concatenate([seg_values, other_values], 0),
                jnp.concatenate([other_values, seg_values], 0),
            )
        scores = (
            jnp.einsum("qhd,khd->hqk", slide_query, seg_keys, preferred_element_type=jnp.float32)
            * scaling
        )
        row_max = jnp.max(scores, axis=-1, keepdims=True)
        weights = jnp.exp(scores - row_max)
        totals = jnp.sum(weights, axis=-1)
        level_out = jnp.einsum(
            "hqk,khd->qhd",
            weights.astype(jnp.bfloat16),
            seg_values,
            preferred_element_type=jnp.float32,
        )
        level_outs.append(level_out / jnp.transpose(totals)[..., None])
        level_lses.append(jnp.transpose(row_max[..., 0] + jnp.log(totals)))
        level_masks.append(local_ids[:, None] % dilation == head_ids[None, :] % dilation)
    stacked_lse = jnp.stack(level_lses)
    stacked_masks = jnp.stack(level_masks)
    stacked_outs = jnp.stack(level_outs)
    best_lse = jnp.max(jnp.where(stacked_masks, stacked_lse, -jnp.inf), axis=0)
    factors = jnp.where(stacked_masks, jnp.exp(stacked_lse - best_lse[None]), 0.0)
    mixed_heads = (
        jnp.sum(factors[..., None] * stacked_outs, axis=0) / jnp.sum(factors, axis=0)[..., None]
    )
    mixed_heads = mixed_heads.astype(jnp.bfloat16).reshape(tile_count, slide_width)
    out_proj = add_products((mixed_heads,), (lax.all_gather(w_so, "seq", axis=0, tiled=True),))[0]
    return (own_rows.astype(jnp.float32) + out_proj).astype(jnp.bfloat16)


def solution(mesh):
    placed = (
        P(("groups", "seq"), None, None),
        P(),
        P("seq", None),
        P("seq", None),
        P("seq", None),
        P("seq", None),
        P(),
        P("seq", None),
        P("groups"),
        P(),
        P("seq", None),
        P("seq", None),
        P("seq", None),
        P("seq", None),
    )
    return jax.shard_map(
        shards, mesh=mesh, in_specs=placed, out_specs=P(("groups", "seq"), None), check_vma=False
    )
```

profile of v0, /device:TPU:0, one launch (start us, length us, event | category | flops | bytes accessed | tf_op | source)
XLA Modules:
  0.0 402.0 jit_solution(10852027901165927906)
XLA Ops:
  6.6 0.7 all-gather.12.cloned.1.call-update
  7.3 0.7 all-gather.14.cloned.1.call-update
  8.1 0.7 all-gather.10.cloned.1.call-update
  8.8 0.5 all-gather.16.cloned.1.call-update
  9.4 0.5 all-gather.18.cloned.1.call-update
  10.0 0.5 all-gather.22.cloned.1.call-update
  10.6 0.7 all-gather.24.cloned.1.call-update
  11.3 0.7 all-gather.20.cloned.1.call-update
  12.1 0.7 all-gather.26.cloned.1.call-update
  12.8 2.1 convert_reduce_fusion.1
  14.9 0.5 fusion.2
  15.8 0.5 fusion.4
  16.4 0.8 broadcast_compare_fusion
  17.2 0.5 pad.78.clone
  17.7 36.9 %all-gather.12.cloned.1.call-done = bf16[1536,768]{1,0:T(8,128)(2,1)} async-done(((bf16[96,768]{1,0:T(8,128)(2,1)}), bf16[1536,768]{1,0:T(8,128)(2,1)}) %all-gather.12.cloned.1.call-update) | async-done | bytes 2359312 | tf_op jit(solution)/shard_map/all_gather | solution.py:66
  54.6 4.0 convolution_convert_fusion.1
  58.6 2.7 reshape.402
  61.3 36.6 %all-gather.14.cloned.1.call-done = bf16[1536,768]{1,0:T(8,128)(2,1)} async-done(((bf16[96,768]{1,0:T(8,128)(2,1)}), bf16[1536,768]{1,0:T(8,128)(2,1)}) %all-gather.14.cloned.1.call-update) | async-done | bytes 2359312 | tf_op jit(solution)/shard_map/all_gather | solution.py:67
  97.9 3.5 convolution_convert_fusion
  101.5 2.3 reshape.403
  103.8 37.5 %all-gather.10.cloned.1.call-done = bf16[1536,768]{1,0:T(8,128)(2,1)} async-done(((bf16[96,768]{1,0:T(8,128)(2,1)}), bf16[1536,768]{1,0:T(8,128)(2,1)}) %all-gather.10.cloned.1.call-update) | async-done | bytes 2359312 | tf_op jit(solution)/shard_map/all_gather | solution.py:68
  141.2 3.5 convolution_convert_fusion.2
  144.8 2.3 reshape.401
  147.0 2.8 multiply_reduce_fusion
  149.8 1.1 fusion.6
  150.9 0.5 copy-done.1
  151.4 2.9 convert_reduce_fusion.2
  154.5 29.9 %all-gather.16.cloned.1.call-done = bf16[768,1536]{1,0:T(8,128)(2,1)} async-done(((bf16[48,1536]{1,0:T(8,128)(2,1)}), bf16[768,1536]{1,0:T(8,128)(2,1)}) %all-gather.16.cloned.1.call-update) | async-done | bytes 2359312 | tf_op jit(solution)/shard_map/all_gather | solution.py:94
  184.4 3.0 fusion.100
  187.6 39.9 %all-gather.18.cloned.1.call-done = bf16[1536,768]{1,0:T(8,128)(2,1)} async-done(((bf16[96,768]{1,0:T(8,128)(2,1)}), bf16[1536,768]{1,0:T(8,128)(2,1)}) %all-gather.18.cloned.1.call-update) | async-done | bytes 2359312 | tf_op jit(solution)/shard_map/all_gather | solution.py:99
  227.6 2.2 convolution_convert_fusion.6
  229.8 21.6 %all_gather.35 = bf16[512,768]{1,0:T(8,128)(2,1)S(1)} all-gather(bf16[32,768]{1,0:T(8,128)(2,1)S(1)} %convolution_convert_fusion.6), channel_id=1, replica_groups=mesh['groups'=2,'seq'=16] {'seq'}, dimensions={0}, use_global_device_ids=true | all-gather | bytes 835584 | tf_op jit(solution)/shard_map/all_gather | solution.py:103
  251.6 0.6 gather_fusion
  252.7 14.3 %all-gather.22.cloned.1.call-done = bf16[768,768]{1,0:T(8,128)(2,1)} async-done(((bf16[48,768]{1,0:T(8,128)(2,1)}), bf16[768,768]{1,0:T(8,128)(2,1)}) %all-gather.22.cloned.1.call-update) | async-done | bytes 1179664 | tf_op jit(solution)/shard_map/all_gather | solution.py:118
  267.0 1.6 convolution_convert_fusion.4
  269.0 37.7 %all-gather.24.cloned.1.call-done = bf16[768,768]{1,0:T(8,128)(2,1)} async-done(((bf16[48,768]{1,0:T(8,128)(2,1)}), bf16[768,768]{1,0:T(8,128)(2,1)}) %all-gather.24.cloned.1.call-update) | async-done | bytes 1179664 | tf_op jit(solution)/shard_map/all_gather | solution.py:119
  306.7 1.6 convolution_convert_fusion.3
  310.0 36.3 %all-gather.20.cloned.1.call-done = bf16[768,768]{1,0:T(8,128)(2,1)} async-done(((bf16[48,768]{1,0:T(8,128)(2,1)}), bf16[768,768]{1,0:T(8,128)(2,1)}) %all-gather.20.cloned.1.call-update) | async-done | bytes 1179664 | tf_op jit(solution)/shard_map/all_gather | solution.py:117
  346.3 1.6 convolution_convert_fusion.5
  348.1 0.8 reshape.405
  349.7 0.8 collective-permute-start.6
  350.6 1.4 collective-permute-start.15
  352.0 0.8 collective-permute-start.3
  352.8 1.4 collective-permute-done.6
  354.3 0.6 collective-permute-start.12
  355.2 0.9 collective-permute-start.7
  356.2 1.2 collective-permute-start.16
  357.5 1.4 collective-permute-start.1
  359.5 0.8 collective-permute-start.10
  360.4 1.6 collective-permute-done.12
  362.1 0.7 collective-permute-start.4
  363.4 1.4 collective-permute-start.13
  364.9 0.9 collective-permute-start.8
  365.8 1.0 maximum_select_fusion.17
  366.8 0.9 collective-permute-done.1
  367.7 1.3 collective-permute-start.17
  369.2 1.3 fusion.103
  370.8 1.6 collective-permute-done.10
  373.0 10.0 %collective-permute-done.4 = bf16[64,12,64]{2,1,0:T(8,128)(2,1)S(1)} collective-permute-done((bf16[64,12,64]{2,1,0:T(8,128)(2,1)S(1)}, bf16[64,12,64]{2,1,0:T(8,128)(2,1)S(1)}, u32[]{:S(2)}, u32[]{:S(2)}) %collective-permute-start.4) | collective-permute-done | bytes 98336 | tf_op jit(solution)/shard_map/ppermute | solution.py:18
  383.3 4.8 %collective-permute-done.13 = bf16[64,12,64]{2,1,0:T(8,128)(2,1)S(1)} collective-permute-done((bf16[64,12,64]{2,1,0:T(8,128)(2,1)S(1)}, bf16[64,12,64]{2,1,0:T(8,128)(2,1)S(1)}, u32[]{:S(2)}, u32[]{:S(2)}) %collective-permute-start.13) | collective-permute-done | bytes 98336 | tf_op jit(solution)/shard_map/ppermute | solution.py:18
  388.5 0.4 fusion.102
  389.5 1.4 fusion.101
  391.3 1.3 fusion.16
  393.3 2.2 fusion.21
  (125 shorter events, 9.9 us)
Async XLA Ops:
  6.5 8.4 %copy-start = (bf16[32,16,1536]{2,1,0:T(8,128)(2,1)S(1)}, bf16[32,16,1536]{2,1,0:T(8,128)(2,1)}, u32[]{:S(2)}) copy-start(bf16[32,16,1536]{2,1,0:T(8,128)(2,1)} %param.14) | copy-start | bytes 4718596
  6.5 8.9 %copy-start.8 = (bf16[1536]{0:T(1024)(128)(2,1)S(1)}, bf16[1536]{0:T(1024)(128)(2,1)}, u32[]{:S(2)}) copy-start(bf16[1536]{0:T(1024)(128)(2,1)} %param.15) | copy-start | bytes 9220
  6.5 8.9 %copy-start.9 = (bf16[1536]{0:T(1024)(128)(2,1)S(1)}, bf16[1536]{0:T(1024)(128)(2,1)}, u32[]{:S(2)}) copy-start(bf16[1536]{0:T(1024)(128)(2,1)} %param.20) | copy-start | bytes 9220
  6.5 9.0 %copy-start.12 = (s32[128]{0:T(128)S(1)}, s32[128]{0:T(128)}, u32[]{:S(2)}) copy-start(s32[128]{0:T(128)} %param.22) | copy-start | bytes 1540
  6.5 9.2 %copy-start.11 = (bf16[768]{0:T(1024)(128)(2,1)S(1)}, bf16[768]{0:T(1024)(128)(2,1)}, u32[]{:S(2)}) copy-start(bf16[768]{0:T(1024)(128)(2,1)} %param.23) | copy-start | bytes 4612
  6.5 48.1 %all-gather.12.cloned.1.call-start = ((), (), s32[]{:S(2)}) async-start(), calls=%async_computation.1 | async-start | bytes 2506752 | tf_op jit(solution)/shard_map/all_gather | solution.py:66
  7.3 90.6 %all-gather.14.cloned.1.call-start = ((), (), s32[]{:S(2)}) async-start(), calls=%async_computation.2 | async-start | bytes 2506752 | tf_op jit(solution)/shard_map/all_gather | solution.py:67
  8.0 133.2 %all-gather.10.cloned.1.call-start = ((), (), s32[]{:S(2)}) async-start(), calls=%async_computation | async-start | bytes 2506752 | tf_op jit(solution)/shard_map/all_gather | solution.py:68
  8.8 175.6 %all-gather.16.cloned.1.call-start = ((), (), s32[]{:S(2)}) async-start(), calls=%async_computation.3 | async-start | bytes 2506752 | tf_op jit(solution)/shard_map/all_gather | solution.py:94
  9.3 218.2 %all-gather.18.cloned.1.call-start = ((), (), s32[]{:S(2)}) async-start(), calls=%async_computation.4 | async-start | bytes 2506752 | tf_op jit(solution)/shard_map/all_gather | solution.py:99
  9.9 257.1 %all-gather.22.cloned.1.call-start = ((), (), s32[]{:S(2)}) async-start(), calls=%async_computation.6 | async-start | bytes 1253376 | tf_op jit(solution)/shard_map/all_gather | solution.py:118
  10.5 296.2 %all-gather.24.cloned.1.call-start = ((), (), s32[]{:S(2)}) async-start(), calls=%async_computation.7 | async-start | bytes 1253376 | tf_op jit(solution)/shard_map/all_gather | solution.py:119
  11.3 335.0 %all-gather.20.cloned.1.call-start = ((), (), s32[]{:S(2)}) async-start(), calls=%async_computation.5 | async-start | bytes 1253376 | tf_op jit(solution)/shard_map/all_gather | solution.py:117
  12.0 381.3 %all-gather.26.cloned.1.call-start = ((), (), s32[]{:S(2)}) async-start(), calls=%async_computation.8 | async-start | bytes 1253376 | tf_op jit(solution)/shard_map/all_gather | solution.py:172
  15.8 330.5 %copy-start.6 = (pred[32]{0:T(512)(128)(4,1)}, pred[32]{0:T(512)(128)(4,1)S(1)}, u32[]{:S(2)}) copy-start(pred[32]{0:T(512)(128)(4,1)S(1)} %broadcast_in_dim.113) | copy-start | bytes 100
  16.4 38.2 %copy-start.2 = (bf16[32,16,1536]{2,1,0:T(8,128)(2,1)}, bf16[32,16,1536]{2,1,0:T(8,128)(2,1)S(1)}, u32[]{:S(2)}) copy-start(bf16[32,16,1536]{2,1,0:T(8,128)(2,1)S(1)} %fusion.4) | copy-start | bytes 4718596
  149.8 1.6 copy-start.1
  308.9 40.5 %collective-permute-start.5 = (bf16[8,12,64]{2,1,0:T(8,128)(2,1)S(1)}, bf16[8,12,64]{2,1,0:T(8,128)(2,1)S(1)}, u32[]{:S(2)}, u32[]{:S(2)}) collective-permute-start(bf16[8,12,64]{2,1,0:T(8,128)(2,1)S(1)} %get-tuple-element.9), channel_id=1, source_target_pairs={{0,1},{1,0},{2,3},{3,2},{4,5},{5,4},{6,7},{7,6},{8,9},{9,8},{10,11... | collective-permute-start | bytes 36872 | tf_op jit(solution)/shard_map/ppermute | solution.py:18
  309.4 46.8 %collective-permute-start = (bf16[32,12,64]{2,1,0:T(8,128)(2,1)S(1)}, bf16[32,12,64]{2,1,0:T(8,128)(2,1)S(1)}, u32[]{:S(2)}, u32[]{:S(2)}) collective-permute-start(bf16[32,12,64]{2,1,0:T(8,128)(2,1)S(1)} %reshape_reshape.18), channel_id=1, source_target_pairs={{0,1},{1,0},{2,3},{3,2},{4,5},{5,4},{6,7},{7,6},{8,9},{9,8},{10,11... | collective-permute-start | bytes 147464 | tf_op jit(solution)/shard_map/ppermute | solution.py:18
  309.7 40.0 %collective-permute-start.14 = (bf16[8,12,64]{2,1,0:T(8,128)(2,1)S(1)}, bf16[8,12,64]{2,1,0:T(8,128)(2,1)S(1)}, u32[]{:S(2)}, u32[]{:S(2)}) collective-permute-start(bf16[8,12,64]{2,1,0:T(8,128)(2,1)S(1)} %get-tuple-element.10), channel_id=1, source_target_pairs={{0,1},{1,0},{2,3},{3,2},{4,5},{5,4},{6,7},{7,6},{8,9},{9,8},{10,11... | collective-permute-start | bytes 36872 | tf_op jit(solution)/shard_map/ppermute | solution.py:18
  348.9 1.7 collective-permute-start.2
  349.2 8.3 %collective-permute-start.9 = (bf16[32,12,64]{2,1,0:T(8,128)(2,1)S(1)}, bf16[32,12,64]{2,1,0:T(8,128)(2,1)S(1)}, u32[]{:S(2)}, u32[]{:S(2)}) collective-permute-start(bf16[32,12,64]{2,1,0:T(8,128)(2,1)S(1)} %reshape_reshape.21), channel_id=1, source_target_pairs={{0,1},{1,0},{2,3},{3,2},{4,5},{5,4},{6,7},{7,6},{8,9},{9,8},{10,11... | collective-permute-start | bytes 147464 | tf_op jit(solution)/shard_map/ppermute | solution.py:18
  349.4 2.6 collective-permute-start.11
  349.7 4.5 %collective-permute-start.6 = (bf16[16,12,64]{2,0,1:T(8,128)(2,1)S(1)}, bf16[16,12,64]{2,0,1:T(8,128)(2,1)S(1)}, u32[]{:S(2)}, u32[]{:S(2)}) collective-permute-start(bf16[16,12,64]{2,0,1:T(8,128)(2,1)S(1)} %maximum_select_fusion.22), channel_id=1, source_target_pairs={{0,2},{1,3},{2,0},{3,1},{4,6},{5,7},{6,4},{7,5},{8,10},{9,11},{10,... | collective-permute-start | bytes 73736 | tf_op jit(solution)/shard_map/ppermute | solution.py:18
  350.6 4.7 %collective-permute-start.15 = (bf16[16,12,64]{2,0,1:T(8,128)(2,1)S(1)}, bf16[16,12,64]{2,0,1:T(8,128)(2,1)S(1)}, u32[]{:S(2)}, u32[]{:S(2)}) collective-permute-start(bf16[16,12,64]{2,0,1:T(8,128)(2,1)S(1)} %maximum_select_fusion.23), channel_id=1, source_target_pairs={{0,2},{1,3},{2,0},{3,1},{4,6},{5,7},{6,4},{7,5},{8,10},{9,11},{10,... | collective-permute-start | bytes 73736 | tf_op jit(solution)/shard_map/ppermute | solution.py:18
  352.0 7.5 %collective-permute-start.3 = (bf16[32,12,64]{2,1,0:T(8,128)(2,1)S(1)}, bf16[32,12,64]{2,1,0:T(8,128)(2,1)S(1)}, u32[]{:S(2)}, u32[]{:S(2)}) collective-permute-start(bf16[32,12,64]{2,1,0:T(8,128)(2,1)S(1)} %maximum_select_fusion.18), channel_id=1, source_target_pairs={{0,2},{1,3},{2,0},{3,1},{4,6},{5,7},{6,4},{7,5},{8,10},{9,11},{10,... | collective-permute-start | bytes 147464 | tf_op jit(solution)/shard_map/ppermute | solution.py:18
  354.3 7.8 %collective-permute-start.12 = (bf16[32,12,64]{2,1,0:T(8,128)(2,1)S(1)}, bf16[32,12,64]{2,1,0:T(8,128)(2,1)S(1)}, u32[]{:S(2)}, u32[]{:S(2)}) collective-permute-start(bf16[32,12,64]{2,1,0:T(8,128)(2,1)S(1)} %maximum_select_fusion.19), channel_id=1, source_target_pairs={{0,2},{1,3},{2,0},{3,1},{4,6},{5,7},{6,4},{7,5},{8,10},{9,11},{10,... | collective-permute-start | bytes 147464 | tf_op jit(solution)/shard_map/ppermute | solution.py:18
  355.2 8.2 %collective-permute-start.7 = (bf16[32,12,64]{2,0,1:T(8,128)(2,1)S(1)}, bf16[32,12,64]{2,0,1:T(8,128)(2,1)S(1)}, u32[]{:S(2)}, u32[]{:S(2)}) collective-permute-start(bf16[32,12,64]{2,0,1:T(8,128)(2,1)S(1)} %maximum_select_fusion.20), channel_id=1, source_target_pairs={{0,4},{1,5},{2,6},{3,7},{4,0},{5,1},{6,2},{7,3},{8,12},{9,13},{10,... | collective-permute-start | bytes 147464 | tf_op jit(solution)/shard_map/ppermute | solution.py:18
  356.2 8.7 %collective-permute-start.16 = (bf16[32,12,64]{2,0,1:T(8,128)(2,1)S(1)}, bf16[32,12,64]{2,0,1:T(8,128)(2,1)}, u32[]{:S(2)}, u32[]{:S(2)}) collective-permute-start(bf16[32,12,64]{2,0,1:T(8,128)(2,1)S(1)} %maximum_select_fusion.21), channel_id=1, source_target_pairs={{0,4},{1,5},{2,6},{3,7},{4,0},{5,1},{6,2},{7,3},{8,12},{9,13},{10,... | collective-permute-start | bytes 147464 | tf_op jit(solution)/shard_map/ppermute | solution.py:18
  357.5 10.2 %collective-permute-start.1 = (bf16[64,12,64]{2,1,0:T(8,128)(2,1)S(1)}, bf16[64,12,64]{2,1,0:T(8,128)(2,1)S(1)}, u32[]{:S(2)}, u32[]{:S(2)}) collective-permute-start(bf16[64,12,64]{2,1,0:T(8,128)(2,1)S(1)} %maximum_select_fusion.4), channel_id=1, source_target_pairs={{0,2},{1,3},{2,0},{3,1},{4,6},{5,7},{6,4},{7,5},{8,10},{9,11},{10,... | collective-permute-start | bytes 294920 | tf_op jit(solution)/shard_map/ppermute | solution.py:18
  359.5 12.9 %collective-permute-start.10 = (bf16[64,12,64]{2,1,0:T(8,128)(2,1)S(1)}, bf16[64,12,64]{2,1,0:T(8,128)(2,1)S(1)}, u32[]{:S(2)}, u32[]{:S(2)}) collective-permute-start(bf16[64,12,64]{2,1,0:T(8,128)(2,1)S(1)} %maximum_select_fusion.6), channel_id=1, source_target_pairs={{0,2},{1,3},{2,0},{3,1},{4,6},{5,7},{6,4},{7,5},{8,10},{9,11},{10,... | collective-permute-start | bytes 294920 | tf_op jit(solution)/shard_map/ppermute | solution.py:18
  362.1 21.0 %collective-permute-start.4 = (bf16[64,12,64]{2,1,0:T(8,128)(2,1)S(1)}, bf16[64,12,64]{2,1,0:T(8,128)(2,1)S(1)}, u32[]{:S(2)}, u32[]{:S(2)}) collective-permute-start(bf16[64,12,64]{2,1,0:T(8,128)(2,1)S(1)} %maximum_select_fusion.5), channel_id=1, source_target_pairs={{0,4},{1,5},{2,6},{3,7},{4,0},{5,1},{6,2},{7,3},{8,12},{9,13},{10,... | collective-permute-start | bytes 294920 | tf_op jit(solution)/shard_map/ppermute | solution.py:18
  363.4 24.8 %collective-permute-start.13 = (bf16[64,12,64]{2,1,0:T(8,128)(2,1)S(1)}, bf16[64,12,64]{2,1,0:T(8,128)(2,1)S(1)}, u32[]{:S(2)}, u32[]{:S(2)}) collective-permute-start(bf16[64,12,64]{2,1,0:T(8,128)(2,1)S(1)} %maximum_select_fusion.7), channel_id=1, source_target_pairs={{0,4},{1,5},{2,6},{3,7},{4,0},{5,1},{6,2},{7,3},{8,12},{9,13},{10,... | collective-permute-start | bytes 294920 | tf_op jit(solution)/shard_map/ppermute | solution.py:18
  364.9 24.6 %collective-permute-start.8 = (bf16[64,12,64]{2,0,1:T(8,128)(2,1)S(1)}, bf16[64,12,64]{2,0,1:T(8,128)(2,1)}, u32[]{:S(2)}, u32[]{:S(2)}) collective-permute-start(bf16[64,12,64]{2,0,1:T(8,128)(2,1)S(1)} %maximum_select_fusion.12), channel_id=1, source_target_pairs={{0,8},{1,9},{2,10},{3,11},{4,12},{5,13},{6,14},{7,15},{8,0},{9,1},... | collective-permute-start | bytes 294920 | tf_op jit(solution)/shard_map/ppermute | solution.py:18
  366.8 21.6 %copy-start.3 = (bf16[32,12,64]{2,1,0:T(8,128)(2,1)S(1)}, bf16[32,12,64]{2,1,0:T(8,128)(2,1)}, u32[]{:S(2)}) copy-start(bf16[32,12,64]{2,1,0:T(8,128)(2,1)} %reshape.405) | copy-start | bytes 147460
  367.7 23.6 %collective-permute-start.17 = (bf16[64,12,64]{2,0,1:T(8,128)(2,1)S(1)}, bf16[64,12,64]{2,0,1:T(8,128)(2,1)}, u32[]{:S(2)}, u32[]{:S(2)}) collective-permute-start(bf16[64,12,64]{2,0,1:T(8,128)(2,1)S(1)} %maximum_select_fusion.17), channel_id=1, source_target_pairs={{0,8},{1,9},{2,10},{3,11},{4,12},{5,13},{6,14},{7,15},{8,0},{9,1},... | collective-permute-start | bytes 294920 | tf_op jit(solution)/shard_map/ppermute | solution.py:18
  388.4 2.8 copy-start.4
  388.4 2.8 copy-start.5
  388.4 2.8 copy-start.10
  390.9 2.3 copy-start.7
Sparse Core Ops, SparseCore 0:
  9.7 44.9 all-gather.11
  56.9 40.9 all-gather.13
  100.2 40.9 all-gather.9
  143.4 40.9 all-gather.15
  186.5 40.9 all-gather.17
  229.7 37.2 all-gather.21
  269.3 37.3 all-gather.23
  308.9 37.3 all-gather.19
  348.6 41.7 all-gather.25
where the time goes:
time: 403 us; the launch traced here: 402 us
  waiting for transfers between devices  296 us (73%)
  matrix products  34.3 us (9%)
  blocking collectives  21.6 us (5%)
  starting transfers between devices  14.1 us (3%)
  between operations  13.9 us (3%)
  local copies, waits for them, and re-layouts  13.4 us (3%)
  other arithmetic  9.15 us (2%)
    all_gather x1, waiting for transfers between devices, shards(): lax.all_gather(w_in, 'seq', axis=0, tiled=True)  39.9 us
    all_gather x1, waiting for transfers between devices, shards(): lax.all_gather(w_sv, 'seq', axis=0, tiled=True)  37.7 us
    all_gather x1, waiting for transfers between devices, shards(): lax.all_gather(w_value, 'seq', axis=0, tiled=True)  37.5 us
    all_gather x1, waiting for transfers between devices, shards(): lax.all_gather(w_query, 'seq', axis=0, tiled=True)  36.9 us
    all_gather x1, waiting for transfers between devices, shards(): lax.all_gather(w_key, 'seq', axis=0, tiled=True)  36.6 us
    all_gather x1, waiting for transfers between devices, shards(): lax.all_gather(w_sq, 'seq', axis=0, tiled=True)  36.3 us
    all_gather x1, waiting for transfers between devices, shards(): lax.all_gather(w_out, 'seq', axis=0, tiled=True).astype(jnp.float32)  29.9 us
    all_gather x1, blocking collectives, shards(): gathered = lax.all_gather(embedding, 'seq', axis=0, tiled=True)  21.6 us
  transfers between devices with their start and end apart: 27, of which 15 were waited for; matrix products, arithmetic and copies ran while one was open for 13% of the time, Pallas kernels for 0%

commit v1 on v0

--- a/solution.py
+++ b/solution.py
@@ -1,6 +1,8 @@
 import jax
 import jax.numpy as jnp
 from jax import lax
+from jax.experimental import pallas as pl
+from jax.experimental.pallas import tpu as pltpu
 from jax.sharding import PartitionSpec as P
 
 HT = 12
@@ -40,7 +42,7 @@
     )
 
 
-def shards(
+def shards_by_gathers(
     tiles,
     tile_gain,
     w_query,
@@ -173,7 +175,396 @@
     return (own_rows.astype(jnp.float32) + out_proj).astype(jnp.bfloat16)
 
 
+MESH = pl.DeviceIdType.MESH
+f32, bf16 = jnp.float32, jnp.bfloat16
+
+
+def iota(shape, dim):
+    return lax.broadcasted_iota(jnp.int32, shape, dim)
+
+
+def dot(a, b):
+    return jnp.dot(a, b, preferred_element_type=f32)
+
+
+def dot_t(a, b):
+    return lax.dot_general(a, b, (((1,), (1,)), ((), ())), preferred_element_type=f32)
+
+
+def attend(query, keys, values, mask=None):
+    scores = dot_t(query, keys) * scaling
+    if mask is not None:
+        scores = jnp.where(mask, scores, -1e30)
+    row_max = jnp.max(scores, axis=-1, keepdims=True)
+    weights = jnp.exp(scores - row_max)
+    if mask is not None:
+        weights = jnp.where(mask, weights, 0.0)
+    totals = jnp.sum(weights, axis=-1, keepdims=True)
+    return dot(weights.astype(bf16), values) / totals, row_max + jnp.log(totals)
+
+
+CHUNKS = (
+    (0, 0, 384), (1, 0, 384), (2, 0, 384), (0, 384, 384), (1, 384, 384), (2, 384, 384),
+    (3, 0, 768), (3, 768, 768), (4, 0, 384), (4, 384, 384), (5, 0, 768),
+)
+NCH = len(CHUNKS)
+LINE = 4
+SEQ = 16
+LEAD = 2
+
+
+def slab_kernel(
+    tiles, tile_gain, w_query, w_key, w_value, w_out, pool_gain, w_in, block_order, slide_gain,
+    w_sq, w_sk, w_sv, w_so, out,
+    *scratch,
+):
+    bufs = scratch[:NCH]
+    (normed, tq, tk, tv, att, emb, stage, wslide, perm, snorm, sq, sk, sv, souts, slses, mixp,
+     msend, mrecv, mcat, own_rows,
+     zs, zr, ys, yr, xs, xr, cs, cr, es, er, ws, wr, ms, mr) = scratch[NCH:]
+    sources = (w_query, w_key, w_value, w_out, w_in, w_so)
+    x = lax.axis_index("groups")
+    me = lax.axis_index("seq")
+    z = me // 4
+    y = (me // 2) % 2
+    c = me % 2
+    at_y = {"seq": z * 4 + (1 - y) * 2 + c}
+    at_c = {"seq": z * 4 + y * 2 + (1 - c)}
+    at_x = {"groups": 1 - x}
+
+    barrier = pltpu.get_barrier_semaphore()
+    for o in range(1, SEQ):
+        pl.semaphore_signal(barrier, inc=1, device_id={"seq": lax.rem(me + o, SEQ)}, device_id_type=MESH)
+    pl.semaphore_signal(barrier, inc=1, device_id=at_x, device_id_type=MESH)
+
+    for k, (w, first, cols) in enumerate(CHUNKS):
+        bufs[k][z, y, c] = sources[w][:, first:first + cols]
+    pl.semaphore_wait(barrier, SEQ)
+
+    def copy(source, target, send, recv, device):
+        return pltpu.make_async_remote_copy(
+            src_ref=source, dst_ref=target, send_sem=send, recv_sem=recv,
+            device_id=device, device_id_type=MESH,
+        )
+
+    def line_copy(k, way, s):
+        block = z - (s - 1) if way == 0 else z + (s - 1)
+        device = {"seq": me + 4} if way == 0 else {"seq": me - 4}
+        valid = jnp.logical_and(z >= s - 1, z < LINE - 1) if way == 0 else jnp.logical_and(z <= LINE - s, z > 0)
+        ref = bufs[k].at[block, y, c]
+        n = way * 3 + s - 1
+        return valid, copy(ref, ref, zs.at[k, n], zr.at[k, n], device)
+
+    def line_send(k, s):
+        for way in (0, 1):
+            valid, remote = line_copy(k, way, s)
+            pl.when(valid)(remote.start)
+
+    def line_wait_send(k, s):
+        for way in (0, 1):
+            valid, remote = line_copy(k, way, s)
+            pl.when(valid)(remote.wait_send)
+
+    def line_wait(k, s):
+        for way in (0, 1):
+            valid = z >= s if way == 0 else z <= LINE - 1 - s
+            block = z - s if way == 0 else z + s
+            n = way * 3 + s - 1
+            ref = bufs[k].at[block, y, c]
+            pl.when(valid)(copy(ref, ref, zs.at[k, n], zr.at[k, n], {"seq": me}).wait_recv)
+
+    def half(k, which_y, core, g):
+        rows, cols = bufs[k].shape[3:]
+        if rows % 32 == 0:
+            return bufs[k].at[:, which_y, core, pl.ds(pl.multiple_of(g * (rows // 2), 16), rows // 2), :]
+        return bufs[k].at[:, which_y, core, :, pl.ds(pl.multiple_of(g * (cols // 2), 128), cols // 2)]
+
+    def y_copy(k):
+        ref = half(k, y, c, x)
+        return copy(ref, ref, ys.at[k], yr.at[k], at_y)
+
+    def x_copy(k):
+        ref = half(k, 1 - y, c, x)
+        return copy(ref, ref, xs.at[k], xr.at[k], at_x)
+
+    def c_copy(k, n):
+        ref = bufs[k].at[:, y if n == 0 else 1 - y, c]
+        return copy(ref, ref, cs.at[k, n], cr.at[k, n], at_c)
+
+    def step(k, st):
+        if st == 0:
+            line_send(k, 1)
+        elif st == 1:
+            line_wait(k, 1)
+            line_send(k, 2)
+        elif st == 2:
+            line_wait(k, 2)
+            line_send(k, 3)
+        elif st == 3:
+            line_wait(k, 3)
+            y_copy(k).start()
+            c_copy(k, 0).start()
+        elif st == 4:
+            y_copy(k).wait_recv()
+            x_copy(k).start()
+        elif st == 5:
+            x_copy(k).wait_recv()
+            c_copy(k, 1).start()
+        else:
+            c_copy(k, 0).wait_recv()
+            c_copy(k, 1).wait_recv()
+
+    def tick(t):
+        if t + LEAD < NCH:
+            step(t + LEAD, 0)
+        for st in range(6, 0, -1):
+            if 0 <= t - st < NCH:
+                step(t - st, st)
+
+    def weight(k):
+        rows, cols = bufs[k].shape[3:]
+        return bufs[k][...].reshape(SEQ * rows, cols)
+
+    def norm_piece(first, rows):
+        @pl.loop(first, first + rows, step=64)
+        def _(r):
+            at = pl.ds(pl.multiple_of(r, 64), 64)
+            normed[at, :] = norm_rows(tiles[at, :], tile_gain[...]).astype(bf16)
+
+    def project(k, ref):
+        @pl.loop(0, 512, step=128)
+        def _(r):
+            at = pl.ds(pl.multiple_of(r, 128), 128)
+            ref[at, :] = dot(normed[at, :], weight(k)).astype(bf16)
+
+    def tile_attention(part):
+        mask = iota((128, 128), 0) // 16 == iota((128, 128), 1) // 16
+
+        @pl.loop(0, 512, step=128)
+        def _(r):
+            at = pl.ds(pl.multiple_of(r, 128), 128)
+            for pair in range(3):
+                outs = []
+                for h in (2 * pair, 2 * pair + 1):
+                    cols = slice(h * 64, h * 64 + 64)
+                    outs.append(attend(tq[at, cols], tk[at, cols], tv[at, cols], mask)[0])
+                first = part * 384 + pair * 128
+                att[at, first:first + 128] = jnp.concatenate(outs, axis=1).astype(bf16)
+
+    def stage_slide():
+        for h in range(HS):
+            stage[h] = jnp.concatenate([w[:, h * 64:h * 64 + 64] for w in (w_sq, w_sk, w_sv)], axis=1)
+
+        @pl.when(me < HS)
+        def _():
+            wslide[me] = stage[me]
+
+    def w_copy(o, device, block):
+        return copy(stage.at[block], wslide.at[me], ws.at[o], wr.at[o], {"seq": device})
+
+    def slide_send(wait):
+        for o in range(1, SEQ):
+            d = lax.rem(me + o, SEQ)
+            @pl.when(d < HS)
+            def _():
+                remote = w_copy(o, d, d)
+                remote.wait_send() if wait else remote.start()
+
+    def slide_wait():
+        @pl.when(me < HS)
+        def _():
+            for o in range(1, SEQ):
+                source = lax.rem(me + SEQ - o, SEQ)
+                copy(stage.at[0], wslide.at[source], ws.at[o], wr.at[o], {"seq": me}).wait_recv()
+
+    def source_rows(position):
+        rows = position.shape[0]
+        table = block_order[...].astype(f32)
+        hot = iota((rows, 128), 1) == position[:, :1] // 4
+        block = jnp.sum(jnp.where(hot, table, 0.0), axis=1, keepdims=True)
+        source = block.astype(jnp.int32) * 4 + position[:, :1] % 4
+        return (iota((rows, 512), 1) == source).astype(f32).astype(bf16)
+
+    def build_perm():
+        for j in range(4):
+            perm[j * 128:j * 128 + 128, :] = source_rows(iota((128, 128), 0) * 4 + j)
+
+    for k in range(LEAD):
+        step(k, 0)
+    done = {}
+    for t in range(NCH + 6):
+        tick(t)
+        if t < 4:
+            norm_piece(t * 128, 128)
+        if t == 4:
+            stage_slide()
+        if t == 5:
+            build_perm()
+        if t == NCH - LEAD:
+            slide_send(False)
+        if t in (6, 9):
+            project(t - 6, tq)
+        if t in (7, 10):
+            project(t - 6, tk)
+        if t in (8, 11):
+            project(t - 6, tv)
+            tile_attention((t - 6) // 3)
+        if t == 11:
+            gather16 = (iota((32, 512), 1) // 16 == iota((32, 512), 0)).astype(f32).astype(bf16)
+            token_mean = dot(gather16, tiles[...]) * (1.0 / 16.0)
+            mean = dot(gather16, att[...]) * (1.0 / 16.0)
+            high = mean.astype(bf16)
+            low = (mean - high.astype(f32)).astype(bf16)
+            both = jnp.concatenate([high, low], axis=0)
+        if t in (12, 13):
+            product = dot(both, weight(t - 6))
+            done[t] = product[:32] + product[32:]
+        if t == 13:
+            pooled = token_mean + jnp.concatenate([done[12], done[13]], axis=1)
+            pooled_norm = norm_rows(pooled, pool_gain[...]).astype(bf16)
+        if t == 14:
+            emb[z, y, c, :, :384] = dot(pooled_norm, weight(8)).astype(bf16)
+        if t == 15:
+            emb[z, y, c, :, 384:] = dot(pooled_norm, weight(9)).astype(bf16)
+            def e_copy(n, d, ref):
+                return copy(ref, ref, es.at[n], er.at[n], d)
+            sends = []
+            for o in range(1, LINE):
+                sends.append(e_copy(o, {"seq": lax.rem(me + 4 * o, SEQ)}, emb.at[z, y, c]))
+                sends[-1].start()
+    for o in range(1, LINE):
+        e_copy(o, {"seq": me}, emb.at[lax.rem(z + LINE - o, LINE), y, c]).wait_recv()
+    to_y = e_copy(0, at_y, emb.at[:, y, c])
+    to_y.start()
+    to_c = e_copy(4, at_c, emb.at[:, y, c])
+    to_c.start()
+    slide_wait()
+    to_y.wait_recv()
+    to_c2 = e_copy(5, at_c, emb.at[:, 1 - y, c])
+    to_c2.start()
+    to_c.wait_recv()
+    to_c2.wait_recv()
+
+    every = emb[...].reshape(512, 768)
+    own_rows[...] = dot(source_rows(iota((32, 128), 0) + me * 32), every)
+
+    @pl.when(me < HS)
+    def _():
+        @pl.loop(0, 512, step=128)
+        def _(r):
+            at = pl.ds(pl.multiple_of(r, 128), 128)
+            ordered = dot(perm[at, :], every)
+            rows = norm_rows(ordered, slide_gain[...]).astype(bf16)
+            projected = dot(rows, wslide[...].reshape(768, 192)).astype(bf16)
+            sq[at, :] = projected[:, :64]
+            sk[at, :] = projected[:, 64:128]
+            sv[at, :] = projected[:, 128:]
+
+        for level in (1, 2):
+            slses[level] = jnp.full((512, 64), -1e30, f32)
+            souts[level] = jnp.zeros((512, 64), f32)
+
+        def level_attention(level, pieces):
+            def rows(ref):
+                return jnp.concatenate([ref[at, :] for at in pieces], axis=0)
+            result, lse = attend(rows(sq), rows(sk), rows(sv))
+            lse = jnp.broadcast_to(lse, result.shape)
+            size = 128 // len(pieces)
+            for n, at in enumerate(pieces):
+                souts[level, at, :] = result[n * size:n * size + size]
+                slses[level, at, :] = lse[n * size:n * size + size]
+
+        for s in range(4):
+            level_attention(0, [pl.ds(j * 128 + 32 * s, 32) for j in range(4)])
+        even = (me % 2) * 128
+        for s in range(2):
+            level_attention(1, [pl.ds(pl.multiple_of(even + j * 256 + 64 * s, 64), 64) for j in range(2)])
+        level_attention(2, [pl.ds(pl.multiple_of((me % 4) * 128, 128), 128)])
+        best = jnp.maximum(jnp.maximum(slses[0], slses[1]), slses[2])
+        total = jnp.zeros((512, 64), f32)
+        mixed = jnp.zeros((512, 64), f32)
+        for level in range(3):
+            factor = jnp.exp(slses[level] - best)
+            total = total + factor
+            mixed = mixed + factor * souts[level]
+        mixed = (mixed / total).astype(bf16)
+        rows, cols = iota((512, 512), 0), iota((512, 512), 1)
+        back = (cols == (rows % 4) * 128 + rows // 4).astype(f32).astype(bf16)
+        msend[...] = dot(back, mixed).astype(bf16).reshape(SEQ, 32, 64)
+        mrecv[me] = msend[me]
+        for o in range(1, SEQ):
+            d = lax.rem(me + o, SEQ)
+            copy(msend.at[d], mrecv.at[me], ms.at[o], mr.at[o], {"seq": d}).start()
+
+    for o in range(1, SEQ):
+        source = lax.rem(me + SEQ - o, SEQ)
+        pl.when(source < HS)(copy(msend.at[0], mrecv.at[jnp.minimum(source, HS - 1)], ms.at[o], mr.at[o], {"seq": me}).wait_recv)
+    for h in range(HS):
+        mcat[:, h * 64:h * 64 + 64] = mrecv[h]
+    out[...] = (own_rows[...] + dot(mcat[...], weight(10))).astype(bf16)
+
+    @pl.when(me < HS)
+    def _():
+        for o in range(1, SEQ):
+            d = lax.rem(me + o, SEQ)
+            copy(msend.at[d], mrecv.at[me], ms.at[o], mr.at[o], {"seq": d}).wait_send()
+    slide_send(True)
+    for remote in sends + [to_y, to_c, to_c2]:
+        remote.wait_send()
+    for k in range(NCH):
+        for s in range(1, LINE):
+            line_wait_send(k, s)
+        y_copy(k).wait_send()
+        x_copy(k).wait_send()
+        c_copy(k, 0).wait_send()
+        c_copy(k, 1).wait_send()
+
+
+def shards_in_kernel(tiles, tile_gain, w_query, w_key, w_value, w_out, pool_gain, w_in, block_order,
+                     slide_gain, w_sq, w_sk, w_sv, w_so):
+    weights = (w_query, w_key, w_value, w_out, w_in, w_so)
+    vmem, dma = pltpu.VMEM, pltpu.SemaphoreType.DMA
+    scratch = [vmem((LINE, 2, 2, weights[w].shape[0], cols), bf16) for w, _, cols in CHUNKS]
+    scratch += [
+        vmem((512, 1536), bf16),
+        vmem((512, 384), bf16), vmem((512, 384), bf16), vmem((512, 384), bf16),
+        vmem((512, 768), bf16),
+        vmem((LINE, 2, 2, 32, 768), bf16),
+        vmem((HS, 48, 192), bf16), vmem((SEQ, 48, 192), bf16),
+        vmem((512, 512), bf16),
+        vmem((16, 128), bf16),
+        vmem((512, 64), bf16), vmem((512, 64), bf16), vmem((512, 64), bf16),
+        vmem((3, 512, 64), f32), vmem((3, 512, 64), f32),
+        vmem((16, 128), bf16),
+        vmem((SEQ, 32, 64), bf16), vmem((HS, 32, 64), bf16), vmem((32, 768), bf16),
+        vmem((32, 768), f32),
+        dma((NCH, 6)), dma((NCH, 6)), dma((NCH,)), dma((NCH,)), dma((NCH,)), dma((NCH,)),
+        dma((NCH, 2)), dma((NCH, 2)), dma((6,)), dma((6,)),
+        dma((SEQ,)), dma((SEQ,)), dma((SEQ,)), dma((SEQ,)),
+    ]
+    return pl.pallas_call(
+        slab_kernel,
+        out_shape=jax.ShapeDtypeStruct((32, 768), bf16),
+        in_specs=[pl.BlockSpec(memory_space=pltpu.VMEM)] * 14,
+        out_specs=pl.BlockSpec(memory_space=pltpu.VMEM),
+        scratch_shapes=scratch,
+        compiler_params=pltpu.CompilerParams(
+            collective_id=0, has_side_effects=True, vmem_limit_bytes=56 * 1024 * 1024
+        ),
+        cost_estimate=pl.CostEstimate(flops=6 * 10**9, bytes_accessed=4 * 10**6, transcendentals=10**6),
+        name="slab",
+    )(
+        tiles.reshape(512, 1536), tile_gain.reshape(1, -1), w_query, w_key, w_value, w_out,
+        pool_gain.reshape(1, -1), w_in, block_order.reshape(1, -1), slide_gain.reshape(1, -1),
+        w_sq, w_sk, w_sv, w_so,
+    )
+
+
 def solution(mesh):
+    shards = shards_by_gathers
+    if mesh.shape['groups'] == 2 and mesh.shape['seq'] == 16:
+        shards = shards_in_kernel
+
     placed = (
         P(("groups", "seq"), None, None),
         P(),

time: 403 us -> 119 us (0.30)
  waiting for transfers between devices: 296 us -> 0 us
  Pallas kernels: 0 us -> 114 us
  matrix products: 34.3 us -> 0 us
  blocking collectives: 21.6 us -> 0 us
  starting transfers between devices: 14.1 us -> 0 us
  between operations: 13.9 us -> 0.01 us
  other arithmetic: 9.15 us -> 0 us
  local copies, waits for them, and re-layouts: 13.4 us -> 5.26 us
    all_gather x9 -> x0, waiting for transfers between devices: 269 us -> none  [the longest x1 39.9 us: shards(): lax.all_gather(w_in, 'seq', axis=0, tiled=True)]
    pallas_call x0 -> x1, Pallas kernels: none -> 114 us  [shards_in_kernel(): pl.pallas_call(slab_kernel, out_shape=jax.ShapeDtypeStruct((32, 768), bf1...]
    dot_general x17 -> x0, matrix products: 34.3 us -> none  [the longest x8 20.4 us: add_products(): jnp.dot(operand, weight_rows, preferred_element_type=jnp.float32)]
    all_gather x1 -> x0, blocking collectives: 21.6 us -> none  [shards(): gathered = lax.all_gather(embedding, 'seq', axis=0, tiled=True)]
    ppermute x18 -> x0, waiting for transfers between devices: 20.8 us -> none  [partner(): return lax.ppermute(value, axis, pairs)]
    ppermute x18 -> x0, starting transfers between devices: 13.7 us -> none  [partner(): return lax.ppermute(value, axis, pairs)]
    unnamed x9 -> x0, waiting for transfers between devices: 5.71 us -> none
    reduce_sum x13 -> x0, other arithmetic: 5.63 us -> none  [the longest x1 2.09 us: shards(): token_mean = jnp.mean(tiles, axis=1, dtype=jnp.float32)]
  transfers between devices with their start and end apart: 27 -> 0, of which waited for: 15 -> 0; matrix products, arithmetic and copies ran while one was open for 13% -> 0% of each run, Pallas kernels for 0% -> 0%
where the time goes in v1:
time: 119 us
  Pallas kernels  114 us (96%)
  local copies, waits for them, and re-layouts  5.26 us (4%)
    pallas_call x1, Pallas kernels, shards_in_kernel(): pl.pallas_call(slab_kernel, out_shape=jax.ShapeDtypeStruct((32, 768), bf1...  114 us

profile of v1, /device:TPU:0, one launch (start us, length us, event | category | flops | bytes accessed | tf_op | source)
XLA Modules:
  0.0 118.8 jit_solution(12285569260268821332)
XLA Ops:
  0.0 1.3 %reshape.19.slide_gain = bf16[1,768]{1,0:T(2,128)(2,1)} reshape(bf16[768]{0:T(1024)(128)(2,1)} %param.23) | data formatting | bytes 3072 | tf_op jit(solution)/shard_map/reshape | solution.py:558
  1.3 1.3 %reshape.16.tile_gain = bf16[1,1536]{1,0:T(2,128)(2,1)} reshape(bf16[1536]{0:T(1024)(128)(2,1)} %param.15) | data formatting | bytes 6144 | tf_op jit(solution)/shard_map/reshape | solution.py:557
  2.6 1.3 %reshape.17.pool_gain = bf16[1,1536]{1,0:T(2,128)(2,1)} reshape(bf16[1536]{0:T(1024)(128)(2,1)} %param.20) | data formatting | bytes 6144 | tf_op jit(solution)/shard_map/reshape | solution.py:558
  3.8 113.5 %slab.1 = bf16[32,768]{1,0:T(8,128)(2,1)} custom-call(bf16[512,1536]{1,0:T(8,128)(2,1)} %bitcast.2, bf16[1,1536]{1,0:T(2,128)(2,1)} %reshape.16.tile_gain, bf16[96,768]{1,0:T(8,128)(2,1)} %w_query.1, bf16[96,768]{1,0:T(8,128)(2,1)} %w_key.1, bf16[96,768]{1,0:T(8,128)(2,1)} %w_value.1, bf16[48,1536]{1,0:T(8,128)(2,1)} %w_out.1, ...), custom_call_target="tpu_custom_call" | custom-call | flops 6000000000 | bytes 4000000 | tf_op jit(solution)/shard_map/slab/pallas_call | solution.py:545
  117.4 1.4 %copy.16 = bf16[32,768]{1,0:T(8,128)(2,1)} copy(bf16[32,768]{1,0:T(8,128)(2,1)} %slab.1) | data formatting | bytes 98304

commit v2 on v1

--- a/solution.py
+++ b/solution.py
@@ -219,7 +219,7 @@
     *scratch,
 ):
     bufs = scratch[:NCH]
-    (normed, tq, tk, tv, att, emb, stage, wslide, perm, snorm, sq, sk, sv, souts, slses, mixp,
+    (normed, tq, tk, tv, att, emb, stage, wslide, perm, sq, sk, sv, souts, slses,
      msend, mrecv, mcat, own_rows,
      zs, zr, ys, yr, xs, xr, cs, cr, es, er, ws, wr, ms, mr) = scratch[NCH:]
     sources = (w_query, w_key, w_value, w_out, w_in, w_so)
@@ -317,7 +317,7 @@
     def tick(t):
         if t + LEAD < NCH:
             step(t + LEAD, 0)
-        for st in range(6, 0, -1):
+        for st in range(1, 7):
             if 0 <= t - st < NCH:
                 step(t - st, st)
 
@@ -337,19 +337,16 @@
             at = pl.ds(pl.multiple_of(r, 128), 128)
             ref[at, :] = dot(normed[at, :], weight(k)).astype(bf16)
 
-    def tile_attention(part):
+    def tile_attention(part, r):
         mask = iota((128, 128), 0) // 16 == iota((128, 128), 1) // 16
-
-        @pl.loop(0, 512, step=128)
-        def _(r):
-            at = pl.ds(pl.multiple_of(r, 128), 128)
-            for pair in range(3):
-                outs = []
-                for h in (2 * pair, 2 * pair + 1):
-                    cols = slice(h * 64, h * 64 + 64)
-                    outs.append(attend(tq[at, cols], tk[at, cols], tv[at, cols], mask)[0])
-                first = part * 384 + pair * 128
-                att[at, first:first + 128] = jnp.concatenate(outs, axis=1).astype(bf16)
+        at = slice(r * 128, r * 128 + 128)
+        for pair in range(3):
+            outs = []
+            for h in (2 * pair, 2 * pair + 1):
+                cols = slice(h * 64, h * 64 + 64)
+                outs.append(attend(tq[part, at, cols], tk[part, at, cols], tv[part, at, cols], mask)[0])
+            first = part * 384 + pair * 128
+            att[at, first:first + 128] = jnp.concatenate(outs, axis=1).astype(bf16)
 
     def stage_slide():
         for h in range(HS):
@@ -389,10 +386,41 @@
         for j in range(4):
             perm[j * 128:j * 128 + 128, :] = source_rows(iota((128, 128), 0) * 4 + j)
 
+    def e_copy(n, part, device, ref):
+        ref = ref.at[..., pl.ds(384 * part, 384)]
+        return copy(ref, ref, es.at[part, n], er.at[part, n], device)
+
+    sends = []
+
+    def emb_part(part):
+        emb[z, y, c, :, 384 * part:384 * part + 384] = dot(pooled_norm, weight(8 + part)).astype(bf16)
+        for o in range(1, LINE):
+            sends.append(e_copy(o, part, {"seq": lax.rem(me + 4 * o, SEQ)}, emb.at[z, y, c]))
+            sends[-1].start()
+
+    def emb_line_wait(part):
+        for o in range(1, LINE):
+            e_copy(o, part, {"seq": me}, emb.at[lax.rem(z + LINE - o, LINE), y, c]).wait_recv()
+        sends.append(e_copy(0, part, at_y, emb.at[:, y, c]))
+        sends[-1].start()
+        sends.append(e_copy(4, part, at_c, emb.at[:, y, c]))
+        sends[-1].start()
+
+    def emb_y_wait(part):
+        e_copy(0, part, at_y, emb.at[:, 1 - y, c]).wait_recv()
+        sends.append(e_copy(5, part, at_c, emb.at[:, 1 - y, c]))
+        sends[-1].start()
+
+    def emb_wait(part):
+        e_copy(4, part, at_c, emb.at[:, y, 1 - c]).wait_recv()
+        e_copy(5, part, at_c, emb.at[:, 1 - y, 1 - c]).wait_recv()
+
     for k in range(LEAD):
         step(k, 0)
-    done = {}
-    for t in range(NCH + 6):
+    pieces = {
+        8: [(0, 0)], 9: [(0, 1)], 10: [(0, 2), (0, 3)], 11: [(1, 0)], 12: [(1, 1), (1, 2)], 13: [(1, 3)],
+    }
+    for t in range(NCH + 5):
         tick(t)
         if t < 4:
             norm_piece(t * 128, 128)
@@ -403,47 +431,35 @@
         if t == NCH - LEAD:
             slide_send(False)
         if t in (6, 9):
-            project(t - 6, tq)
+            project(t - 6, tq.at[(t - 6) // 3])
         if t in (7, 10):
-            project(t - 6, tk)
+            project(t - 6, tk.at[(t - 6) // 3])
         if t in (8, 11):
-            project(t - 6, tv)
-            tile_attention((t - 6) // 3)
-        if t == 11:
+            project(t - 6, tv.at[(t - 6) // 3])
+        for part, r in pieces.get(t, ()):
+            tile_attention(part, r)
+        if t == 12:
             gather16 = (iota((32, 512), 1) // 16 == iota((32, 512), 0)).astype(f32).astype(bf16)
             token_mean = dot(gather16, tiles[...]) * (1.0 / 16.0)
+        if t == 13:
             mean = dot(gather16, att[...]) * (1.0 / 16.0)
             high = mean.astype(bf16)
             low = (mean - high.astype(f32)).astype(bf16)
             both = jnp.concatenate([high, low], axis=0)
-        if t in (12, 13):
-            product = dot(both, weight(t - 6))
-            done[t] = product[:32] + product[32:]
-        if t == 13:
-            pooled = token_mean + jnp.concatenate([done[12], done[13]], axis=1)
+            product = jnp.concatenate([dot(both, weight(6)), dot(both, weight(7))], axis=1)
+            pooled = token_mean + product[:32] + product[32:]
             pooled_norm = norm_rows(pooled, pool_gain[...]).astype(bf16)
         if t == 14:
-            emb[z, y, c, :, :384] = dot(pooled_norm, weight(8)).astype(bf16)
+            emb_part(0)
         if t == 15:
-            emb[z, y, c, :, 384:] = dot(pooled_norm, weight(9)).astype(bf16)
-            def e_copy(n, d, ref):
-                return copy(ref, ref, es.at[n], er.at[n], d)
-            sends = []
-            for o in range(1, LINE):
-                sends.append(e_copy(o, {"seq": lax.rem(me + 4 * o, SEQ)}, emb.at[z, y, c]))
-                sends[-1].start()
-    for o in range(1, LINE):
-        e_copy(o, {"seq": me}, emb.at[lax.rem(z + LINE - o, LINE), y, c]).wait_recv()
-    to_y = e_copy(0, at_y, emb.at[:, y, c])
-    to_y.start()
-    to_c = e_copy(4, at_c, emb.at[:, y, c])
-    to_c.start()
+            emb_part(1)
+            emb_line_wait(0)
+    emb_line_wait(1)
+    emb_y_wait(0)
+    emb_y_wait(1)
     slide_wait()
-    to_y.wait_recv()
-    to_c2 = e_copy(5, at_c, emb.at[:, 1 - y, c])
-    to_c2.start()
-    to_c.wait_recv()
-    to_c2.wait_recv()
+    emb_wait(0)
+    emb_wait(1)
 
     every = emb[...].reshape(512, 768)
     own_rows[...] = dot(source_rows(iota((32, 128), 0) + me * 32), every)
@@ -501,6 +517,7 @@
         pl.when(source < HS)(copy(msend.at[0], mrecv.at[jnp.minimum(source, HS - 1)], ms.at[o], mr.at[o], {"seq": me}).wait_recv)
     for h in range(HS):
         mcat[:, h * 64:h * 64 + 64] = mrecv[h]
+    step(NCH - 1, 6)
     out[...] = (own_rows[...] + dot(mcat[...], weight(10))).astype(bf16)
 
     @pl.when(me < HS)
@@ -509,7 +526,7 @@
             d = lax.rem(me + o, SEQ)
             copy(msend.at[d], mrecv.at[me], ms.at[o], mr.at[o], {"seq": d}).wait_send()
     slide_send(True)
-    for remote in sends + [to_y, to_c, to_c2]:
+    for remote in sends:
         remote.wait_send()
     for k in range(NCH):
         for s in range(1, LINE):
@@ -527,19 +544,17 @@
     scratch = [vmem((LINE, 2, 2, weights[w].shape[0], cols), bf16) for w, _, cols in CHUNKS]
     scratch += [
         vmem((512, 1536), bf16),
-        vmem((512, 384), bf16), vmem((512, 384), bf16), vmem((512, 384), bf16),
+        vmem((2, 512, 384), bf16), vmem((2, 512, 384), bf16), vmem((2, 512, 384), bf16),
         vmem((512, 768), bf16),
         vmem((LINE, 2, 2, 32, 768), bf16),
         vmem((HS, 48, 192), bf16), vmem((SEQ, 48, 192), bf16),
         vmem((512, 512), bf16),
-        vmem((16, 128), bf16),
         vmem((512, 64), bf16), vmem((512, 64), bf16), vmem((512, 64), bf16),
         vmem((3, 512, 64), f32), vmem((3, 512, 64), f32),
-        vmem((16, 128), bf16),
         vmem((SEQ, 32, 64), bf16), vmem((HS, 32, 64), bf16), vmem((32, 768), bf16),
         vmem((32, 768), f32),
         dma((NCH, 6)), dma((NCH, 6)), dma((NCH,)), dma((NCH,)), dma((NCH,)), dma((NCH,)),
-        dma((NCH, 2)), dma((NCH, 2)), dma((6,)), dma((6,)),
+        dma((NCH, 2)), dma((NCH, 2)), dma((2, 6)), dma((2, 6)),
         dma((SEQ,)), dma((SEQ,)), dma((SEQ,)), dma((SEQ,)),
     ]
     return pl.pallas_call(
@@ -554,8 +569,8 @@
         cost_estimate=pl.CostEstimate(flops=6 * 10**9, bytes_accessed=4 * 10**6, transcendentals=10**6),
         name="slab",
     )(
-        tiles.reshape(512, 1536), tile_gain.reshape(1, -1), w_query, w_key, w_value, w_out,
-        pool_gain.reshape(1, -1), w_in, block_order.reshape(1, -1), slide_gain.reshape(1, -1),
+        tiles.reshape(512, 1536), tile_gain, w_query, w_key, w_value, w_out,
+        pool_gain, w_in, block_order.reshape(1, -1), slide_gain,
         w_sq, w_sk, w_sv, w_so,
     )
 

time: 119 us -> 103 us (0.87)
  Pallas kernels: 114 us -> 101 us
  local copies, waits for them, and re-layouts: 5.26 us -> 1.42 us
    pallas_call x1, Pallas kernels: 114 us -> 101 us  [shards_in_kernel(): pl.pallas_call(slab_kernel, out_shape=jax.ShapeDtypeStruct((32, 768), bf1...]
    reshape x3 -> x0, local copies, waits for them, and re-layouts: 3.84 us -> none  [the longest x1 1.28 us: shards_in_kernel(): tile_gain.reshape(1, -1)]
where the time goes in v2:
time: 103 us
  Pallas kernels  101 us (98%)
  local copies, waits for them, and re-layouts  1.42 us (1%)
    pallas_call x1, Pallas kernels, shards_in_kernel(): pl.pallas_call(slab_kernel, out_shape=jax.ShapeDtypeStruct((32, 768), bf1...  101 us

profile of v2, /device:TPU:0, one launch (start us, length us, event | category | flops | bytes accessed | tf_op | source)
XLA Modules:
  0.0 102.6 jit_solution(15339274359707757563)
XLA Ops:
  0.0 101.1 %slab.1 = bf16[32,768]{1,0:T(8,128)(2,1)} custom-call(bf16[512,1536]{1,0:T(8,128)(2,1)} %bitcast.2, bf16[1536]{0:T(1024)(128)(2,1)} %tile_gain.1, bf16[96,768]{1,0:T(8,128)(2,1)} %w_query.1, bf16[96,768]{1,0:T(8,128)(2,1)} %w_key.1, bf16[96,768]{1,0:T(8,128)(2,1)} %w_value.1, bf16[48,1536]{1,0:T(8,128)(2,1)} %w_out.1, bf16[1536]{0:T(1024)(128)(2,1)} %pool_gain.1, ...), custom_call_target="tpu_custom_call" | custom-call | flops 6000000000 | bytes 4000000 | tf_op jit(solution)/shard_map/slab/pallas_call | solution.py:560
  101.1 1.4 %copy.16 = bf16[32,768]{1,0:T(8,128)(2,1)} copy(bf16[32,768]{1,0:T(8,128)(2,1)} %slab.1) | data formatting | bytes 98304
